TPU v7x, 32 devices: a whole 2x2x4 slice. The times are simulated.
32 devices in a mesh: wide: 8 (over z, x), narrow: 4 (over y, core).
Axes of the slice: x: 2, y: 2, z: 4, core: 2. Of those that a mesh axis runs over, the one named last changes fastest.
Arguments:
- design: float32 [65536, 128], P(('wide', 'narrow')), may hold values from 0.05 to 1
- filter_tiles: float32 [5, 128, 128], replicated
- filter_cols: int32 [65536, 5], P(('wide', 'narrow')), may hold values from -1 to 65535, as said below
- slot_block: int32 [65536], P(('wide', 'narrow')), may hold values from 0 to 65535, as said below
- holes: int32 [1024, 8192], P('wide', 'narrow'), may hold values 0 or 1
- squeeze_source: float32 [1024, 8192], P('wide', 'narrow'), may hold values from -6 to 6
- force_weight: float32 [1024, 8192], P('wide', 'narrow'), may hold values from 0.2 to 2
Outputs:
- pressure: float32 [1024, 8192], P('wide', 'narrow')
- sensitivity: float32 [65536, 128], P(('wide', 'narrow'))
Inputs may be any that keep to these rules, and one draw needn't show every extreme that they name: `slot_block`: film blocks are ordered along a curve that visits the tiles in order and, inside a tile of 16 x 128 blocks, the blocks in Morton order (column bit lowest); for one stagger h with 512 <= h <= 1536, design slot s controls the block at curve position (s + h) mod 65536. So the slots of owner d (slots d * 2048 to (d + 1) * 2048 - 1) lie in tiles d and d + 1, those of the last owner in its own tile and tile 0. filter_cols[r, 0] = r; entries 1 to 4 are the design slots of the film blocks above, below, left and right of the block of slot r inside the same tile, -1 where that neighbour lies outside the tile.
All inputs are finite; a program needn't handle non-finite values. No bound on the sum of `holes` on one device may be relied on, other than what follows from the above.
Results may differ from a plain program's by a relative error of at most 0.00025.
Values sent between devices are 32-bit elements; how exact they have to be, the bound alone decides.
A program may use at most 192 MiB of HBM per device.

v0:
```python
import jax
import jax.numpy as jnp
from jax import lax
from jax.sharding import PartitionSpec as P

SWEEPS = 16


COND_FLOOR = 0.01
SQUEEZE_DAMPING = 0.25
FULL_PRECISION = lax.Precision.HIGHEST


def extended_2(x, sides, width, wrap):
    for axis, dim in sides:
        size, length = (lax.axis_size(axis), x.shape[dim])
        up = [(i, (i + 1) % size) for i in range(size if wrap else size - 1)]
        down = [(j, i) for i, j in up]
        last = lax.slice_in_dim(x, length - width, length, axis=dim)
        first = lax.slice_in_dim(x, 0, width, axis=dim)
        before = lax.ppermute(last, axis, up)
        after = lax.ppermute(first, axis, down)
        x = jnp.concatenate([before, x, after], axis=dim)
    return x


def passed_along(x, axis, by):
    length = lax.axis_size(axis)
    return lax.ppermute(x, axis, [(i, (i + by) % length) for i in range(length)])


def relax(fields, conduct, sources, solid_mask, rim_depth, outer_rim):
    offset = outer_rim - rim_depth + 1
    inner_rows = fields.shape[1] - 2
    inner_cols = fields.shape[2] - 2

    def window(values, row_step, col_step):
        return values[
            ...,
            offset + row_step : offset + row_step + inner_rows,
            offset + col_step : offset + col_step + inner_cols,
        ]

    k_here = window(conduct, 0, 0)
    face_north = 0.5 * (k_here + window(conduct, -1, 0))
    face_south = 0.5 * (k_here + window(conduct, 1, 0))
    face_west = 0.5 * (k_here + window(conduct, 0, -1))
    face_east = 0.5 * (k_here + window(conduct, 0, 1))
    coupled = face_north * fields[:, 0:inner_rows, 1 : inner_cols + 1]
    coupled = coupled + face_south * fields[:, 2 : inner_rows + 2, 1 : inner_cols + 1]
    coupled = coupled + face_west * fields[:, 1 : inner_rows + 1, 0:inner_cols]
    coupled = coupled + face_east * fields[:, 1 : inner_rows + 1, 2 : inner_cols + 2]
    diagonal = face_north + face_south + face_west + face_east + SQUEEZE_DAMPING
    return (window(sources, 0, 0) + coupled) / diagonal * window(solid_mask, 0, 0)


def film_gradient(padded, density):
    row_count = padded.shape[1] - 2
    col_count = padded.shape[2] - 2
    p_here = padded[0, 1 : row_count + 1, 1 : col_count + 1]
    a_here = padded[1, 1 : row_count + 1, 1 : col_count + 1]
    summed = jnp.zeros((row_count, col_count), jnp.float32)
    for row_start, col_start in ((0, 1), (2, 1), (1, 0), (1, 2)):
        nearby = padded[:, row_start : row_start + row_count, col_start : col_start + col_count]
        summed = summed + (a_here - nearby[1]) * (p_here - nearby[0])
    return -0.5 * summed * (3.0 * (1.0 - COND_FLOOR)) * density * density


def to_tile(blocks, row_count, col_count):
    shaped = blocks.reshape(row_count // 8, col_count // 16, 8, 16)
    return shaped.transpose(0, 2, 1, 3).reshape(row_count, col_count)


def to_blocks(tile):
    row_count, col_count = tile.shape
    shaped = tile.reshape(row_count // 8, 8, col_count // 16, 16)
    return shaped.transpose(0, 2, 1, 3).reshape(-1, 128)


def local(design, filter_tiles, filter_cols, slot_block, holes, squeeze_source, force_weight):
    owned = design.shape[0]
    owners = lax.axis_size(("wide", "narrow"))
    total_slots = owned * owners
    first_slot = lax.axis_index(("wide", "narrow")) * owned
    extended = extended_2(design, ((("wide", "narrow"), 0),), owned, True)
    present = filter_cols >= 0
    local_rows = jnp.where(present, jnp.mod(filter_cols - first_slot + owned, total_slots), 0)
    picked = jnp.where(present[:, :, None], extended[local_rows], 0.0)
    numer = jnp.einsum("rkj,kij->ri", picked, filter_tiles, precision=FULL_PRECISION)
    denom = jnp.dot(
        present.astype(jnp.float32), jnp.sum(filter_tiles, axis=2), precision=FULL_PRECISION
    )
    filtered = numer / denom
    relative = jnp.mod(slot_block - first_slot, total_slots)
    in_own = relative < owned
    own_index = jnp.where(in_own, relative, owned)
    next_index = jnp.where(in_own, owned, relative - owned)
    own_blocks = jnp.zeros((owned + 1, 128), jnp.float32).at[own_index].set(filtered)[:owned]
    next_blocks = jnp.zeros((owned + 1, 128), jnp.float32).at[next_index].set(filtered)[:owned]
    arrived = passed_along(next_blocks, ("wide", "narrow"), 1)
    row_count, col_count = holes.shape
    density = to_tile(own_blocks + arrived, row_count, col_count)
    conduct = COND_FLOOR + (1.0 - COND_FLOOR) * density * density * density
    solid_mask = jnp.where(holes > 0, 0.0, 1.0).astype(jnp.float32)
    statics = jnp.stack([conduct, squeeze_source, force_weight, solid_mask])
    initial = jnp.zeros((2, row_count, col_count), jnp.float32)
    grown_static = extended_2(statics, (("wide", 1), ("narrow", 2)), 1, False)

    def single_sweep(sweep_index, fields):
        grown = extended_2(fields, (("wide", 1), ("narrow", 2)), 1, False)
        return relax(grown, grown_static[0], grown_static[1:3], grown_static[3], 1, 1)

    fields = lax.fori_loop(0, SWEEPS, single_sweep, initial)
    padded_final = extended_2(fields, (("wide", 1), ("narrow", 2)), 1, False)
    film_sens = film_gradient(padded_final, density)
    tile_sens = to_blocks(film_sens)
    next_sens = passed_along(tile_sens, ("wide", "narrow"), -1)
    returned = jnp.concatenate([tile_sens, next_sens], axis=0)[relative]
    scaled = returned / denom
    spread = jnp.einsum("ri,kij->rkj", scaled, filter_tiles, precision=FULL_PRECISION)
    spread = jnp.where(present[:, :, None], spread, 0.0)
    collected = jnp.zeros((3 * owned, 128), jnp.float32).at[local_rows].add(spread)
    from_next = passed_along(collected[:owned], ("wide", "narrow"), -1)
    from_prev = passed_along(collected[2 * owned :], ("wide", "narrow"), 1)
    sensitivity = collected[owned : 2 * owned] + from_next + from_prev
    return (fields[0], sensitivity)


def solution(mesh):
    placed = (
        P(("wide", "narrow"), None),
        P(),
        P(("wide", "narrow"), None),
        P(("wide", "narrow")),
        P("wide", "narrow"),
        P("wide", "narrow"),
        P("wide", "narrow"),
    )
    return jax.shard_map(
        local,
        mesh=mesh,
        in_specs=placed,
        out_specs=(P("wide", "narrow"), P(("wide", "narrow"), None)),
        check_vma=False,
    )
```

profile of v0, /device:TPU:9, one launch (start us, length us, event | category | flops | bytes accessed | tf_op | source)
XLA Modules:
  0.0 774.5 jit_solution(10857714572681656294)
XLA Ops:
  6.7 19.1 %collective-permute-done.4 = f32[2048,128]{1,0:T(8,128)S(1)} collective-permute-done((f32[2048,128]{1,0:T(8,128)}, f32[2048,128]{1,0:T(8,128)S(1)}, u32[]{:S(2)}, u32[]{:S(2)}) %collective-permute-start.4) | collective-permute-done | bytes 1048608 | tf_op jit(solution)/shard_map/ppermute | solution.py:21
  30.3 34.5 %gather_fusion = f32[10240,128]{1,0:T(8,128)} fusion(f32[6144,128]{1,0:T(8,128)S(1)} %pad_maximum_fusion.12, s32[10240]{0:T(1024)S(1)} %broadcast_clamp_fusion), kind=kCustom, calls=%fused_computation | custom fusion | bytes 10526720 | tf_op jit(solution)/shard_map/gather | solution.py:88
  64.8 7.4 reshape.83
  72.2 8.6 %fusion.14 = f32[2048,128]{1,0:T(8,128)} fusion(f32[2048,128]{1,0:T(8,128)S(1)} %copy-done.11, f32[5,128,128]{2,1,0:T(8,128)S(1)} %copy-done, f32[2048,5,128]{2,1,0:T(8,128)} %reshape.83, pred[2048,5]{0,1:T(8,128)(4,1)S(1)} %get-tuple-element.85), kind=kOutput, calls=%fused_computation.42 | convolution fusion | flops 2014838784 | bytes 7677952 | tf_op jit(solution)/shard_map/rkj,kij->ri/dot_general | solution.py:89
  107.6 7.9 %reshape.77 = f32[1,128,2048]{2,1,0:T(8,128)S(1)} reshape(f32[16,8,128,16]{3,2,1,0:T(8,128)} %copy.21) | data formatting | bytes 2097152 | tf_op jit(solution)/shard_map/reshape | solution.py:71
  139.4 6.7 concatenate.51
  150.6 445.7 %while.12 = (s32[]{:T(128)}, f32[2,128,2048]{2,1,0:T(8,128)}, f32[4,130,2050]{2,1,0:T(8,128)}, f32[128,2048]{1,0:T(8,128)}, f32[128,2048]{1,0:T(8,128)}, /*index...) while((s32[]{:T(128)}, f32[2,128,2048]{2,1,0:T(8,128)}, ...), condition=%wide.region_4.5_spmd.clone, body=%wide.region_3.4_spmd.clone.sunk | while | flops 12059667 | bytes 57981584 | solution.py:113
  172.9 6.6 fusion.53
  311.8 6.6 fusion.53
  339.6 6.6 fusion.53
  367.4 6.6 fusion.53
  395.2 6.6 fusion.53
  423.0 6.6 fusion.53
  450.7 6.6 fusion.53
  478.5 6.6 fusion.53
  506.3 6.6 fusion.53
  534.1 6.6 fusion.53
  561.9 6.6 fusion.53
  634.9 14.4 %collective-permute-done.15 = f32[2048,128]{1,0:T(8,128)S(1)} collective-permute-done((f32[2048,128]{1,0:T(8,128)}, f32[2048,128]{1,0:T(8,128)S(1)}, u32[]{:S(2)}, u32[]{:S(2)}) %collective-permute-start.15) | collective-permute-done | bytes 1048608 | tf_op jit(solution)/shard_map/ppermute | solution.py:29
  652.1 9.3 %gather_fusion.1 = f32[2048,128]{1,0:T(8,128)} fusion(f32[4096,128]{1,0:T(8,128)} %pad_maximum_fusion.13, s32[2048]{0:T(1024)S(1)} %get-tuple-element.109), kind=kCustom, calls=%fused_computation.1 | custom fusion | bytes 2105344 | tf_op jit(solution)/shard_map/gather | solution.py:118
  667.2 12.9 %copy.25 = f32[2048,5,128]{2,1,0:T(8,128)} copy(f32[2048,5,128]{2,0,1:T(8,128)S(1)} %convolution_select_fusion) | data formatting | bytes 10485760 | tf_op jit(solution)/shard_map/jit(_where)/select_n | solution.py:121
  680.1 7.9 %reshape.118 = f32[10240,128]{1,0:T(8,128)} reshape(f32[2048,5,128]{2,1,0:T(8,128)} %copy.25) | data formatting | bytes 10485760 | tf_op jit(solution)/shard_map/jit(_where)/select_n | solution.py:121
  688.0 56.9 %scatter_custom_fusion.2 = f32[6144,128]{1,0:T(8,128)} fusion(s32[10240]{0:T(1024)} %copy-done.17, f32[10240,128]{1,0:T(8,128)} %reshape.118, f32[]{:T(128)} %constant.31.clone.1), kind=kCustom, calls=%fused_computation.44 | custom fusion | flops 1310720 | bytes 3146240 | tf_op jit(solution)/shard_map/scatter-add | solution.py:122
  749.4 22.7 %collective-permute-done.16 = f32[2048,128]{1,0:T(8,128)S(1)} collective-permute-done((f32[2048,128]{1,0:T(8,128)S(1)}, f32[2048,128]{1,0:T(8,128)S(1)}, u32[]{:S(2)}, u32[]{:S(2)}) %collective-permute-start.16) | collective-permute-done | bytes 1048608 | tf_op jit(solution)/shard_map/ppermute | solution.py:29
  (512 shorter events, 490.9 us)
Async XLA Ops:
  0.7 25.1 %collective-permute-start.4 = (f32[2048,128]{1,0:T(8,128)}, f32[2048,128]{1,0:T(8,128)S(1)}, u32[]{:S(2)}, u32[]{:S(2)}) collective-permute-start(f32[2048,128]{1,0:T(8,128)} %param.9), channel_id=1, source_target_pairs={{0,1},{1,2},{2,3},{3,4},{4,5},{5,6},{6,7},{7,8},{8,9},{9,10},{10,1... | collective-permute-start | bytes 3145736 | tf_op jit(solution)/shard_map/ppermute | solution.py:21
  2.5 25.8 %collective-permute-start.5 = (f32[2048,128]{1,0:T(8,128)}, f32[2048,128]{1,0:T(8,128)}, u32[]{:S(2)}, u32[]{:S(2)}) collective-permute-start(f32[2048,128]{1,0:T(8,128)} %param.9), channel_id=1, source_target_pairs={{1,0},{2,1},{3,2},{4,3},{5,4},{6,5},{7,6},{8,7},{9,8},{10,9},{11,1... | collective-permute-start | bytes 3145736 | tf_op jit(solution)/shard_map/ppermute | solution.py:22
  88.1 12.9 %collective-permute-start.6 = (f32[2048,128]{1,0:T(8,128)}, f32[2048,128]{1,0:T(8,128)}, u32[]{:S(2)}, u32[]{:S(2)}) collective-permute-start(f32[2048,128]{1,0:T(8,128)} %slice.214), channel_id=1, source_target_pairs={{0,1},{1,2},{2,3},{3,4},{4,5},{5,6},{6,7},{7,8},{8,9},{9,10},{10,1... | collective-permute-start | bytes 3145736 | tf_op jit(solution)/shard_map/ppermute | solution.py:29
  128.1 10.0 %collective-permute-start.10 = (f32[4,130,1]{2,1,0:T(8,128)S(1)}, f32[4,130,1]{2,1,0:T(8,128)S(1)}, u32[]{:S(2)}, u32[]{:S(2)}) collective-permute-start(f32[4,130,1]{2,1,0:T(8,128)S(1)} %get-tuple-element.95), channel_id=1, source_target_pairs={{1,0},{2,1},{3,2},{5,4},{6,5},{7,6},{9,8},{10,9},{11,10},{13,12},{... | collective-permute-start | bytes 6248 | tf_op jit(solution)/shard_map/ppermute | solution.py:22
  160.9 11.9 %collective-permute-start.2 = (f32[2,130,1]{2,1,0:T(8,128)}, f32[2,130,1]{2,1,0:T(8,128)}, u32[]{:S(2)}, u32[]{:S(2)}) collective-permute-start(f32[2,130,1]{2,1,0:T(8,128)} %get-tuple-element.166), channel_id=1, source_target_pairs={{1,0},{2,1},{3,2},{5,4},{6,5},{7,6},{9,8},{10,9},{11,10},{13,12},{... | collective-permute-start | bytes 3128 | tf_op jit(solution)/shard_map/while/body/eval_jaxpr/ppermute | solution.py:22
  162.8 10.0 %collective-permute-start.3 = (f32[2,130,1]{2,1,0:T(8,128)}, f32[2,130,1]{2,1,0:T(8,128)}, u32[]{:S(2)}, u32[]{:S(2)}) collective-permute-start(f32[2,130,1]{2,1,0:T(8,128)} %get-tuple-element.167), channel_id=1, source_target_pairs={{0,1},{1,2},{2,3},{4,5},{5,6},{6,7},{8,9},{9,10},{10,11},{12,13},{... | collective-permute-start | bytes 3128 | tf_op jit(solution)/shard_map/while/body/eval_jaxpr/ppermute | solution.py:21
  190.0 10.6 %collective-permute-start.2 = (f32[2,130,1]{2,1,0:T(8,128)}, f32[2,130,1]{2,1,0:T(8,128)}, u32[]{:S(2)}, u32[]{:S(2)}) collective-permute-start(f32[2,130,1]{2,1,0:T(8,128)} %get-tuple-element.166), channel_id=1, source_target_pairs={{1,0},{2,1},{3,2},{5,4},{6,5},{7,6},{9,8},{10,9},{11,10},{13,12},{... | collective-permute-start | bytes 3128 | tf_op jit(solution)/shard_map/while/body/eval_jaxpr/ppermute | solution.py:22
  218.1 10.2 %collective-permute-start.2 = (f32[2,130,1]{2,1,0:T(8,128)}, f32[2,130,1]{2,1,0:T(8,128)}, u32[]{:S(2)}, u32[]{:S(2)}) collective-permute-start(f32[2,130,1]{2,1,0:T(8,128)} %get-tuple-element.166), channel_id=1, source_target_pairs={{1,0},{2,1},{3,2},{5,4},{6,5},{7,6},{9,8},{10,9},{11,10},{13,12},{... | collective-permute-start | bytes 3128 | tf_op jit(solution)/shard_map/while/body/eval_jaxpr/ppermute | solution.py:22
  246.0 10.2 %collective-permute-start.2 = (f32[2,130,1]{2,1,0:T(8,128)}, f32[2,130,1]{2,1,0:T(8,128)}, u32[]{:S(2)}, u32[]{:S(2)}) collective-permute-start(f32[2,130,1]{2,1,0:T(8,128)} %get-tuple-element.166), channel_id=1, source_target_pairs={{1,0},{2,1},{3,2},{5,4},{6,5},{7,6},{9,8},{10,9},{11,10},{13,12},{... | collective-permute-start | bytes 3128 | tf_op jit(solution)/shard_map/while/body/eval_jaxpr/ppermute | solution.py:22
  273.8 10.2 %collective-permute-start.2 = (f32[2,130,1]{2,1,0:T(8,128)}, f32[2,130,1]{2,1,0:T(8,128)}, u32[]{:S(2)}, u32[]{:S(2)}) collective-permute-start(f32[2,130,1]{2,1,0:T(8,128)} %get-tuple-element.166), channel_id=1, source_target_pairs={{1,0},{2,1},{3,2},{5,4},{6,5},{7,6},{9,8},{10,9},{11,10},{13,12},{... | collective-permute-start | bytes 3128 | tf_op jit(solution)/shard_map/while/body/eval_jaxpr/ppermute | solution.py:22
  301.6 10.1 %collective-permute-start.2 = (f32[2,130,1]{2,1,0:T(8,128)}, f32[2,130,1]{2,1,0:T(8,128)}, u32[]{:S(2)}, u32[]{:S(2)}) collective-permute-start(f32[2,130,1]{2,1,0:T(8,128)} %get-tuple-element.166), channel_id=1, source_target_pairs={{1,0},{2,1},{3,2},{5,4},{6,5},{7,6},{9,8},{10,9},{11,10},{13,12},{... | collective-permute-start | bytes 3128 | tf_op jit(solution)/shard_map/while/body/eval_jaxpr/ppermute | solution.py:22
  329.4 10.1 %collective-permute-start.2 = (f32[2,130,1]{2,1,0:T(8,128)}, f32[2,130,1]{2,1,0:T(8,128)}, u32[]{:S(2)}, u32[]{:S(2)}) collective-permute-start(f32[2,130,1]{2,1,0:T(8,128)} %get-tuple-element.166), channel_id=1, source_target_pairs={{1,0},{2,1},{3,2},{5,4},{6,5},{7,6},{9,8},{10,9},{11,10},{13,12},{... | collective-permute-start | bytes 3128 | tf_op jit(solution)/shard_map/while/body/eval_jaxpr/ppermute | solution.py:22
  357.2 10.0 %collective-permute-start.2 = (f32[2,130,1]{2,1,0:T(8,128)}, f32[2,130,1]{2,1,0:T(8,128)}, u32[]{:S(2)}, u32[]{:S(2)}) collective-permute-start(f32[2,130,1]{2,1,0:T(8,128)} %get-tuple-element.166), channel_id=1, source_target_pairs={{1,0},{2,1},{3,2},{5,4},{6,5},{7,6},{9,8},{10,9},{11,10},{13,12},{... | collective-permute-start | bytes 3128 | tf_op jit(solution)/shard_map/while/body/eval_jaxpr/ppermute | solution.py:22
  385.1 10.0 %collective-permute-start.2 = (f32[2,130,1]{2,1,0:T(8,128)}, f32[2,130,1]{2,1,0:T(8,128)}, u32[]{:S(2)}, u32[]{:S(2)}) collective-permute-start(f32[2,130,1]{2,1,0:T(8,128)} %get-tuple-element.166), channel_id=1, source_target_pairs={{1,0},{2,1},{3,2},{5,4},{6,5},{7,6},{9,8},{10,9},{11,10},{13,12},{... | collective-permute-start | bytes 3128 | tf_op jit(solution)/shard_map/while/body/eval_jaxpr/ppermute | solution.py:22
  412.9 10.0 %collective-permute-start.2 = (f32[2,130,1]{2,1,0:T(8,128)}, f32[2,130,1]{2,1,0:T(8,128)}, u32[]{:S(2)}, u32[]{:S(2)}) collective-permute-start(f32[2,130,1]{2,1,0:T(8,128)} %get-tuple-element.166), channel_id=1, source_target_pairs={{1,0},{2,1},{3,2},{5,4},{6,5},{7,6},{9,8},{10,9},{11,10},{13,12},{... | collective-permute-start | bytes 3128 | tf_op jit(solution)/shard_map/while/body/eval_jaxpr/ppermute | solution.py:22
  440.7 9.9 %collective-permute-start.2 = (f32[2,130,1]{2,1,0:T(8,128)}, f32[2,130,1]{2,1,0:T(8,128)}, u32[]{:S(2)}, u32[]{:S(2)}) collective-permute-start(f32[2,130,1]{2,1,0:T(8,128)} %get-tuple-element.166), channel_id=1, source_target_pairs={{1,0},{2,1},{3,2},{5,4},{6,5},{7,6},{9,8},{10,9},{11,10},{13,12},{... | collective-permute-start | bytes 3128 | tf_op jit(solution)/shard_map/while/body/eval_jaxpr/ppermute | solution.py:22
  468.5 9.9 %collective-permute-start.2 = (f32[2,130,1]{2,1,0:T(8,128)}, f32[2,130,1]{2,1,0:T(8,128)}, u32[]{:S(2)}, u32[]{:S(2)}) collective-permute-start(f32[2,130,1]{2,1,0:T(8,128)} %get-tuple-element.166), channel_id=1, source_target_pairs={{1,0},{2,1},{3,2},{5,4},{6,5},{7,6},{9,8},{10,9},{11,10},{13,12},{... | collective-permute-start | bytes 3128 | tf_op jit(solution)/shard_map/while/body/eval_jaxpr/ppermute | solution.py:22
  496.3 9.8 %collective-permute-start.2 = (f32[2,130,1]{2,1,0:T(8,128)}, f32[2,130,1]{2,1,0:T(8,128)}, u32[]{:S(2)}, u32[]{:S(2)}) collective-permute-start(f32[2,130,1]{2,1,0:T(8,128)} %get-tuple-element.166), channel_id=1, source_target_pairs={{1,0},{2,1},{3,2},{5,4},{6,5},{7,6},{9,8},{10,9},{11,10},{13,12},{... | collective-permute-start | bytes 3128 | tf_op jit(solution)/shard_map/while/body/eval_jaxpr/ppermute | solution.py:22
  524.1 9.8 %collective-permute-start.2 = (f32[2,130,1]{2,1,0:T(8,128)}, f32[2,130,1]{2,1,0:T(8,128)}, u32[]{:S(2)}, u32[]{:S(2)}) collective-permute-start(f32[2,130,1]{2,1,0:T(8,128)} %get-tuple-element.166), channel_id=1, source_target_pairs={{1,0},{2,1},{3,2},{5,4},{6,5},{7,6},{9,8},{10,9},{11,10},{13,12},{... | collective-permute-start | bytes 3128 | tf_op jit(solution)/shard_map/while/body/eval_jaxpr/ppermute | solution.py:22
  552.0 9.8 %collective-permute-start.2 = (f32[2,130,1]{2,1,0:T(8,128)}, f32[2,130,1]{2,1,0:T(8,128)}, u32[]{:S(2)}, u32[]{:S(2)}) collective-permute-start(f32[2,130,1]{2,1,0:T(8,128)} %get-tuple-element.166), channel_id=1, source_target_pairs={{1,0},{2,1},{3,2},{5,4},{6,5},{7,6},{9,8},{10,9},{11,10},{13,12},{... | collective-permute-start | bytes 3128 | tf_op jit(solution)/shard_map/while/body/eval_jaxpr/ppermute | solution.py:22
  579.8 9.8 %collective-permute-start.2 = (f32[2,130,1]{2,1,0:T(8,128)}, f32[2,130,1]{2,1,0:T(8,128)}, u32[]{:S(2)}, u32[]{:S(2)}) collective-permute-start(f32[2,130,1]{2,1,0:T(8,128)} %get-tuple-element.166), channel_id=1, source_target_pairs={{1,0},{2,1},{3,2},{5,4},{6,5},{7,6},{9,8},{10,9},{11,10},{13,12},{... | collective-permute-start | bytes 3128 | tf_op jit(solution)/shard_map/while/body/eval_jaxpr/ppermute | solution.py:22
  634.9 14.4 %collective-permute-start.15 = (f32[2048,128]{1,0:T(8,128)}, f32[2048,128]{1,0:T(8,128)S(1)}, u32[]{:S(2)}, u32[]{:S(2)}) collective-permute-start(f32[2048,128]{1,0:T(8,128)} %copy.24), channel_id=1, source_target_pairs={{0,31},{1,0},{2,1},{3,2},{4,3},{5,4},{6,5},{7,6},{8,7},{9,8},{10,9... | collective-permute-start | bytes 3145736 | tf_op jit(solution)/shard_map/ppermute | solution.py:29
  746.6 25.5 %collective-permute-start.16 = (f32[2048,128]{1,0:T(8,128)S(1)}, f32[2048,128]{1,0:T(8,128)S(1)}, u32[]{:S(2)}, u32[]{:S(2)}) collective-permute-start(f32[2048,128]{1,0:T(8,128)S(1)} %get-tuple-element.99), channel_id=1, source_target_pairs={{0,31},{1,0},{2,1},{3,2},{4,3},{5,4},{6,5},{7,6},{8,7},{9,8},{10,9... | collective-permute-start | bytes 3145736 | tf_op jit(solution)/shard_map/ppermute | solution.py:29
  747.5 24.7 %collective-permute-start.17 = (f32[2048,128]{1,0:T(8,128)S(1)}, f32[2048,128]{1,0:T(8,128)S(1)}, u32[]{:S(2)}, u32[]{:S(2)}) collective-permute-start(f32[2048,128]{1,0:T(8,128)S(1)} %get-tuple-element.100), channel_id=1, source_target_pairs={{0,1},{1,2},{2,3},{3,4},{4,5},{5,6},{6,7},{7,8},{8,9},{9,10},{10,1... | collective-permute-start | bytes 3145736 | tf_op jit(solution)/shard_map/ppermute | solution.py:29
  (164 other events, 1161.4 us)
where the time goes:
time: 780 us; the launch traced here: 774 us
  other arithmetic  260 us (33%)
  starting transfers between devices  210 us (27%)
  local copies, waits for them, and re-layouts  204 us (26%)
  waiting for transfers between devices  81 us (10%)
  matrix products  16.4 us (2%)
    ppermute x37, starting transfers between devices, extended_2(): before = lax.ppermute(last, axis, up)  114 us
    mul x16, other arithmetic, relax(): (window(sources, 0, 0) + coupled) / diagonal * window(solid_mask, 0, 0)  105 us
    ppermute x37, starting transfers between devices, extended_2(): after = lax.ppermute(first, axis, down)  94.1 us
    scatter-add x1, other arithmetic, local(): jnp.zeros((3 * owned, 128), jnp.float32).at[local_rows].add(spread)  56.9 us
    ppermute x4, waiting for transfers between devices, passed_along(): lax.ppermute(x, axis, [(i, (i + by) % length) for i in range(length)])  42.8 us
    gather x2, local copies, waits for them, and re-layouts, local(): picked = jnp.where(present[:, :, None], extended[local_rows], 0.0)  41.9 us
    squeeze x16, local copies, waits for them, and re-layouts, single_sweep(): grown_static[3]  41 us
    mul x16, other arithmetic, relax(): face_north = 0.5 * (k_here + window(conduct, -1, 0))  38.3 us
  transfers between devices with their start and end apart: 78, of which 25 were waited for; matrix products, arithmetic and copies ran while one was open for 16% of the time, Pallas kernels for 0%

commit v1 on v0

v1 whole, which is shorter than its diff:
```python
import functools

import jax
import jax.numpy as jnp
from jax import lax
from jax.experimental import pallas as pl
from jax.experimental.pallas import tpu as pltpu
from jax.sharding import PartitionSpec as P

SWEEPS = 16
COND_FLOOR = 0.01
SQUEEZE_DAMPING = 0.25
MESH = pl.DeviceIdType.MESH

SLOTS = 2048
RIM = 24
ROWS = 128
TALL = ROWS + 2 * RIM
STRIPS = 16
WIDE = STRIPS + 1
SENT = 1536
GROUP = 256
GROUPS = SLOTS // GROUP
SENT_GROUPS = SENT // GROUP

DESIGN, ST_L, ST_R, ST_U, ST_D, K_L, K_R, K_U, K_D, BACK = range(10)
COPIES = BACK + SENT_GROUPS


def sub_bit(bit):
    return (lax.broadcasted_iota(jnp.int32, (8, 128), 0) // bit) % 2


def swap_middle(x):
    b1, b2 = sub_bit(2), sub_bit(4)
    moved = jnp.where(b1 == 1, pltpu.roll(x, 6, 0), pltpu.roll(x, 2, 0))
    return jnp.where(b1 == b2, x, moved)


def curve_to_rows(group):
    low = sub_bit(2) == 0
    out = {}
    for r3 in range(2):
        for c3 in range(2):
            for r2 in range(2):
                for r1 in range(2):
                    at = 8 * (r1 + 4 * r2 + 8 * c3 + 16 * r3)
                    a, b = group[at : at + 8], group[at + 16 : at + 24]
                    row = 2 * r1 + 4 * r2 + 8 * r3
                    even = jnp.where(low, a, pltpu.roll(b, 2, 0))
                    odd = jnp.where(low, pltpu.roll(a, 6, 0), b)
                    out[row, c3] = swap_middle(even)
                    out[row + 1, c3] = swap_middle(odd)
    return out


def rows_to_curve(group):
    low = sub_bit(2) == 0
    out = [None] * 32
    for r3 in range(2):
        for c3 in range(2):
            for r2 in range(2):
                for r1 in range(2):
                    row = 2 * r1 + 4 * r2 + 8 * r3
                    at = row * 16 + 8 * c3
                    even = swap_middle(group[at : at + 8])
                    odd = swap_middle(group[at + 16 : at + 24])
                    v = r1 + 4 * r2 + 8 * c3 + 16 * r3
                    out[v] = jnp.where(low, even, pltpu.roll(odd, 2, 0))
                    out[v + 2] = jnp.where(low, pltpu.roll(even, 6, 0), odd)
    return out


def flip_block(x):
    chunk = lax.broadcasted_iota(jnp.int32, (8, 128), 1) // 16
    for bit in (1, 2):
        s, c = sub_bit(bit), (chunk // bit) % 2
        up = pltpu.roll(pltpu.roll(x, 8 - bit, 0), 16 * bit, 1)
        down = pltpu.roll(pltpu.roll(x, bit, 0), 128 - 16 * bit, 1)
        x = jnp.where(s == c, x, jnp.where(c == 1, up, down))
    both = pltpu.roll(pltpu.roll(x, 4, 0), 64, 1)
    return jnp.where(sub_bit(4) == chunk // 4, x, both)


def split(x):
    hi = x.astype(jnp.bfloat16)
    lo = (x - hi.astype(jnp.float32)).astype(jnp.bfloat16)
    return hi, lo


def product(lhs, weights):
    hi, lo = split(lhs)
    full = jnp.dot(hi, weights, preferred_element_type=jnp.float32)
    rest = jnp.dot(lo, weights, preferred_element_type=jnp.float32)
    return full[:, :128] + (full[:, 128:] + (rest[:, :128] + rest[:, 128:]))


def body(
    n_wide, n_narrow,
    slot_ref, design_ref, tiles_ref, holes_ref, squeeze_ref, force_ref,
    pressure_ref, sens_ref,
    ext, blocks, curve, wf, wb, sums, st, st_l, st_r, k_l, k_r,
    cond, dens, wn, ws, ww, we, src, fields, send, recv,
):
    w, n = lax.axis_index("wide"), lax.axis_index("narrow")
    owners = n_wide * n_narrow
    me = w * n_narrow + n
    after = lax.rem(me + 1, owners)
    before = lax.rem(me + owners - 1, owners)
    nxt = (after // n_narrow, lax.rem(after, n_narrow))
    prv = (before // n_narrow, lax.rem(before, n_narrow))
    up = (lax.rem(w + n_wide - 1, n_wide), n)
    down = (lax.rem(w + 1, n_wide), n)
    left = (w, lax.rem(n + n_narrow - 1, n_narrow))
    right = (w, lax.rem(n + 1, n_narrow))
    has_up, has_down = w > 0, w < n_wide - 1
    has_left, has_right = n > 0, n < n_narrow - 1

    barrier = pltpu.get_barrier_semaphore()
    pl.semaphore_signal(barrier, inc=1, device_id=nxt, device_id_type=MESH)
    pl.semaphore_signal(barrier, inc=1, device_id=prv, device_id_type=MESH)
    for there, device in ((has_up, up), (has_down, down), (has_left, left), (has_right, right)):
        @pl.when(there)
        def _():
            pl.semaphore_signal(barrier, inc=1, device_id=device, device_id_type=MESH)
    expected = 2 + sum(jnp.where(t, 1, 0) for t in (has_up, has_down, has_left, has_right))
    pl.semaphore_wait(barrier, expected)

    def remote(which, src_ref, dst_ref, device):
        return pltpu.make_async_remote_copy(
            src_ref=src_ref, dst_ref=dst_ref,
            send_sem=send.at[which], recv_sem=recv.at[which],
            device_id=device, device_id_type=MESH,
        )

    tile_rows = pl.ds(RIM, ROWS)
    top_rows, low_rows = pl.ds(RIM, RIM), pl.ds(ROWS, RIM)
    above_rows, below_rows = pl.ds(0, RIM), pl.ds(RIM + ROWS, RIM)
    design_copy = remote(DESIGN, design_ref.at[pl.ds(SLOTS - SENT, SENT)], ext.at[pl.ds(0, SENT)], nxt)
    st_left = remote(ST_L, st.at[:, 0, tile_rows], st_r, left)
    st_right = remote(ST_R, st.at[:, STRIPS - 1, tile_rows], st_l, right)
    st_up = remote(ST_U, st.at[:, :, top_rows], st.at[:, :, below_rows], up)
    st_down = remote(ST_D, st.at[:, :, low_rows], st.at[:, :, above_rows], down)
    k_left = remote(K_L, cond.at[0, tile_rows], k_r, left)
    k_right = remote(K_R, cond.at[STRIPS - 1, tile_rows], k_l, right)
    k_up = remote(K_U, cond.at[:, top_rows], cond.at[:, below_rows], up)
    k_down = remote(K_D, cond.at[:, low_rows], cond.at[:, above_rows], down)

    def start_pair(first, has_first, second, has_second):
        pl.when(has_first)(first.start)
        pl.when(has_second)(second.start)

    def wait_pair(first, has_first, second, has_second):
        pl.when(has_first)(first.wait_send)
        pl.when(has_second)(second.wait_send)
        pl.when(has_second)(first.wait_recv)
        pl.when(has_first)(second.wait_recv)

    design_copy.start()

    for g in range(STRIPS):
        cols = pl.ds(g * 128, 128)
        st[0, g, tile_rows, :] = squeeze_ref[:, cols]
        st[1, g, tile_rows, :] = force_ref[:, cols]
        st[2, g, tile_rows, :] = jnp.where(holes_ref[:, cols] > 0, 0.0, 1.0).astype(jnp.float32)
    start_pair(st_left, has_left, st_right, has_right)

    ext[pl.ds(SENT, SLOTS), :] = design_ref[...]
    blocks[...] = jnp.zeros(blocks.shape, jnp.float32)
    for k in range(5):
        tile = tiles_ref[k]
        turned = tile.T
        rows = pl.ds(k * 128, 128)
        hi, lo = split(turned)
        wf[rows, pl.ds(0, 128)] = hi
        wf[rows, pl.ds(128, 128)] = lo
        hi, lo = split(tile)
        wb[rows, pl.ds(0, 128)] = hi
        wb[rows, pl.ds(128, 128)] = lo
        sums[pl.ds(k, 1), :] = jnp.sum(turned, axis=0, keepdims=True)

    for there, value in ((has_left, st_l), (has_right, st_r)):
        @pl.when(jnp.logical_not(there))
        def _():
            value[...] = jnp.zeros(value.shape, jnp.float32)
    for there, value in ((has_left, k_l), (has_right, k_r)):
        @pl.when(jnp.logical_not(there))
        def _():
            value[...] = jnp.zeros(value.shape, jnp.float32)
    for there, rows in ((has_up, above_rows), (has_down, below_rows)):
        @pl.when(jnp.logical_not(there))
        def _():
            st[:, :, rows, :] = jnp.zeros((3, WIDE, RIM, 128), jnp.float32)
            cond[:, rows, :] = jnp.zeros((WIDE, RIM, 128), jnp.float32)

    wait_pair(st_left, has_left, st_right, has_right)
    lane = lax.broadcasted_iota(jnp.int32, (ROWS, 128), 1)
    for q in range(3):
        st[q, STRIPS, tile_rows, :] = jnp.where(lane < 64, st_r[q], st_l[q])
    start_pair(st_up, has_up, st_down, has_down)

    first = slot_ref[0]
    block_row, block_col = (first // 128) % 16, first % 128
    stagger = (block_col // 16) * 256
    for level in range(4):
        stagger = stagger + (block_col // 2**level) % 2 * 4**level
        stagger = stagger + (block_row // 2**level) % 2 * (2 * 4**level)

    design_copy.wait()
    offset = SENT - stagger

    def place(c, _):
        group = ext[pl.ds(offset + c * GROUP, GROUP), :]
        for (row, half), value in curve_to_rows(group).items():
            at = pl.multiple_of(8 + 16 * c + 8 * half, 8)
            blocks[1 + row, pl.ds(at, 8), :] = value
        return 0

    lax.fori_loop(0, GROUPS, place, 0)

    def near(c):
        def take(row, col):
            return blocks[pl.ds(1 + row, 16), pl.ds(8 + 16 * c + col, 16), :].reshape(GROUP, 128)
        return take

    def denominator(c, width, count):
        row = lax.broadcasted_iota(jnp.int32, (16, width, 128), 0)
        col = lax.broadcasted_iota(jnp.int32, (16, width, 128), 1) + c * width
        total = jnp.broadcast_to(sums[pl.ds(0, 1), :].reshape(1, 1, 128), row.shape)
        inside = (row > 0, row < 15, col > 0, col < 127)
        for k in range(4):
            total = total + jnp.where(inside[k], sums[pl.ds(k + 1, 1), :].reshape(1, 1, 128), 0.0)
        return total.reshape(count, 128)

    def forward(c, _):
        take = near(c)
        lhs = jnp.concatenate([take(0, 0), take(-1, 0), take(1, 0), take(0, -1), take(0, 1)], axis=1)
        filtered = product(lhs, wf[...]) / denominator(c, 16, GROUP)
        for row in range(16):
            for half in range(2):
                at = row * 16 + 8 * half
                film = flip_block(filtered[at : at + 8])
                dens[2 * c + half, pl.ds(row * 8, 8), :] = film
                cond[2 * c + half, pl.ds(RIM + row * 8, 8), :] = (
                    COND_FLOOR + (1.0 - COND_FLOOR) * film * film * film
                )
        return 0

    lax.fori_loop(0, GROUPS, forward, 0)
    start_pair(k_left, has_left, k_right, has_right)
    wait_pair(k_left, has_left, k_right, has_right)
    cond[STRIPS, tile_rows, :] = jnp.where(lane < 64, k_r[...], k_l[...])
    start_pair(k_up, has_up, k_down, has_down)

    lane8 = lax.broadcasted_iota(jnp.int32, (8, 128), 1)

    def sides(row):
        out = []
        for g in range(WIDE):
            west = pltpu.roll(jnp.where(lane8 == 127, row[g - 1], row[g]), 1, 1)
            east = pltpu.roll(jnp.where(lane8 == 0, row[(g + 1) % WIDE], row[g]), 127, 1)
            out.append((west, east))
        return out

    def coefficients(step, _):
        r = pl.multiple_of(step * 8, 8)
        here = [cond[g, pl.ds(r, 8), :] for g in range(WIDE)]
        beside = sides(here)
        for g in range(WIDE):
            k = here[g]
            north = 0.5 * (k + cond[g, pl.ds(r - 1, 8), :])
            south = 0.5 * (k + cond[g, pl.ds(r + 1, 8), :])
            west = 0.5 * (k + beside[g][0])
            east = 0.5 * (k + beside[g][1])
            inverse = 1.0 / (north + south + west + east + SQUEEZE_DAMPING)
            solid = st[2, g, pl.ds(r, 8), :] > 0.5
            for ref, face in ((wn, north), (ws, south), (ww, west), (we, east)):
                ref[g, pl.ds(r, 8), :] = jnp.where(solid, face * inverse, 0.0)
            for q in range(2):
                value = jnp.where(solid, st[q, g, pl.ds(r, 8), :] * inverse, 0.0)
                src[q, g, pl.ds(r, 8), :] = value
                fields[0, q, g, pl.ds(r, 8), :] = value
        return 0

    lax.fori_loop(4, 18, coefficients, 0)
    wait_pair(st_up, has_up, st_down, has_down)
    wait_pair(k_up, has_up, k_down, has_down)
    lax.fori_loop(1, 4, coefficients, 0)
    lax.fori_loop(18, 21, coefficients, 0)

    def sweep(first_step, last_step):
        def run(index, _):
            old, new = index % 2, (index + 1) % 2

            def one(step, _):
                r = pl.multiple_of(step * 8, 8)
                rows = pl.ds(r, 8)
                here = [[fields[old, q, g, rows, :] for g in range(WIDE)] for q in range(2)]
                beside = [sides(here[q]) for q in range(2)]
                for g in range(WIDE):
                    a, b, c, d = wn[g, rows, :], ws[g, rows, :], ww[g, rows, :], we[g, rows, :]
                    for q in range(2):
                        north = fields[old, q, g, pl.ds(r - 1, 8), :]
                        south = fields[old, q, g, pl.ds(r + 1, 8), :]
                        west, east = beside[q][g]
                        fields[new, q, g, rows, :] = (src[q, g, rows, :] + a * north + b * south) + (
                            c * west + d * east
                        )
                return 0

            lax.fori_loop(first_step, last_step, one, 0)
            return 0

        return run

    lax.fori_loop(0, 7, sweep(1, 21), 0)
    lax.fori_loop(7, SWEEPS - 1, sweep(2, 20), 0)
    last = (SWEEPS - 1) % 2

    def gradient(g, _):
        summed = jnp.zeros((ROWS, 128), jnp.float32)
        p = fields[last, 0, g, tile_rows, :]
        a = fields[last, 1, g, tile_rows, :]
        pressure_ref[:, pl.ds(pl.multiple_of(g * 128, 128), 128)] = p
        for shift in (RIM - 1, RIM + 1):
            rows = pl.ds(shift, ROWS)
            summed = summed + (a - fields[last, 1, g, rows, :]) * (p - fields[last, 0, g, rows, :])
        west, east = lax.rem(g + STRIPS, WIDE), g + 1
        for edge, strip, turn in ((127, west, 1), (0, east, 127)):
            pn = pltpu.roll(jnp.where(lane == edge, fields[last, 0, strip, tile_rows, :], p), turn, 1)
            an = pltpu.roll(jnp.where(lane == edge, fields[last, 1, strip, tile_rows, :], a), turn, 1)
            summed = summed + (a - an) * (p - pn)
        density = dens[g]
        sens = -0.5 * summed * (3.0 * (1.0 - COND_FLOOR)) * density * density
        scale = denominator(g, 8, ROWS)
        at = pl.multiple_of(8 + 8 * g, 8)
        for row in range(16):
            part = slice(row * 8, row * 8 + 8)
            blocks[1 + row, pl.ds(at, 8), :] = flip_block(sens[part]) / scale[part]
        return 0

    lax.fori_loop(0, STRIPS, gradient, 0)

    def back_copy(c):
        return remote(BACK + c, curve.at[pl.ds(c * GROUP, GROUP)], curve.at[pl.ds(SLOTS + c * GROUP, GROUP)], prv)

    def backward(c):
        take = near(c)
        lhs = jnp.concatenate([take(0, 0), take(1, 0), take(-1, 0), take(0, 1), take(0, -1)], axis=1)
        for v, value in enumerate(rows_to_curve(product(lhs, wb[...]))):
            at = c * GROUP + 8 * v
            if not isinstance(at, int):
                at = pl.multiple_of(at, 8)
            curve[pl.ds(at, 8), :] = value

    for c in range(GROUPS):
        backward(c)
        if c < SENT_GROUPS:
            back_copy(c).start()
    for c in range(SENT_GROUPS):
        back_copy(c).wait()

    def give(c, _):
        at = pl.multiple_of(c * GROUP, GROUP)
        sens_ref[pl.ds(at, GROUP), :] = curve[pl.ds(stagger + c * GROUP, GROUP), :]
        return 0

    lax.fori_loop(0, GROUPS, give, 0)


def solution(mesh):
    n_wide, n_narrow = mesh.shape["wide"], mesh.shape["narrow"]
    f32, bf16 = jnp.float32, jnp.bfloat16
    vmem = pl.BlockSpec(memory_space=pltpu.VMEM)

    def local(design, filter_tiles, filter_cols, slot_block, holes, squeeze_source, force_weight):
        strips = (WIDE, TALL, 128)
        return pl.pallas_call(
            functools.partial(body, n_wide, n_narrow),
            out_shape=(
                jax.ShapeDtypeStruct(holes.shape, f32),
                jax.ShapeDtypeStruct(design.shape, f32),
            ),
            in_specs=[pl.BlockSpec(memory_space=pltpu.SMEM)] + [vmem] * 5,
            out_specs=(vmem, vmem),
            scratch_shapes=[
                pltpu.VMEM((SENT + SLOTS + 8, 128), f32),
                pltpu.VMEM((18, 144, 128), f32),
                pltpu.VMEM((SENT + SLOTS + 8, 128), f32),
                pltpu.VMEM((640, 256), bf16),
                pltpu.VMEM((640, 256), bf16),
                pltpu.VMEM((8, 128), f32),
                pltpu.VMEM((3,) + strips, f32),
                pltpu.VMEM((3, ROWS, 128), f32),
                pltpu.VMEM((3, ROWS, 128), f32),
                pltpu.VMEM((ROWS, 128), f32),
                pltpu.VMEM((ROWS, 128), f32),
                pltpu.VMEM(strips, f32),
                pltpu.VMEM((STRIPS, ROWS, 128), f32),
                pltpu.VMEM(strips, f32),
                pltpu.VMEM(strips, f32),
                pltpu.VMEM(strips, f32),
                pltpu.VMEM(strips, f32),
                pltpu.VMEM((2,) + strips, f32),
                pltpu.VMEM((2, 2) + strips, f32),
                pltpu.SemaphoreType.DMA((COPIES,)),
                pltpu.SemaphoreType.DMA((COPIES,)),
            ],
            compiler_params=pltpu.CompilerParams(
                collective_id=0, has_side_effects=True, vmem_limit_bytes=56 * 2**20
            ),
        )(slot_block, design, filter_tiles, holes, squeeze_source, force_weight)

    placed = (
        P(("wide", "narrow"), None),
        P(),
        P(("wide", "narrow"), None),
        P(("wide", "narrow")),
        P("wide", "narrow"),
        P("wide", "narrow"),
        P("wide", "narrow"),
    )
    return jax.shard_map(
        local,
        mesh=mesh,
        in_specs=placed,
        out_specs=(P("wide", "narrow"), P(("wide", "narrow"), None)),
        check_vma=False,
    )
```

time: 780 us -> 153 us (0.20)
  other arithmetic: 260 us -> 0 us
  starting transfers between devices: 210 us -> 0 us
  local copies, waits for them, and re-layouts: 204 us -> 3.36 us
  Pallas kernels: 0 us -> 149 us
  waiting for transfers between devices: 81 us -> 0 us
  matrix products: 16.4 us -> 0 us
    ppermute x78 -> x0, starting transfers between devices: 210 us -> none  [the longest x37 114 us: extended_2(): before = lax.ppermute(last, axis, up)]
    mul x34 -> x0, other arithmetic: 149 us -> none  [the longest x16 105 us: relax(): (window(sources, 0, 0) + coupled) / diagonal * window(solid_mask, 0, 0)]
    pallas_call x0 -> x1, Pallas kernels: none -> 149 us  [local(): pl.pallas_call(functools.partial(body, n_wide, n_narrow), out_shape=(jax....]
    ppermute x78 -> x0, waiting for transfers between devices: 81 us -> none  [the longest x4 42.8 us: passed_along(): lax.ppermute(x, axis, [(i, (i + by) % length) for i in range(length)])]
    scatter-add x1 -> x0, other arithmetic: 56.9 us -> none  [local(): jnp.zeros((3 * owned, 128), jnp.float32).at[local_rows].add(spread)]
    gather x3 -> x0, local copies, waits for them, and re-layouts: 51.2 us -> none  [the longest x2 41.9 us: local(): picked = jnp.where(present[:, :, None], extended[local_rows], 0.0)]
    squeeze x18 -> x0, local copies, waits for them, and re-layouts: 43.4 us -> none  [the longest x16 41 us: single_sweep(): grown_static[3]]
    slice x36 -> x0, local copies, waits for them, and re-layouts: 32.6 us -> none  [the longest x16 28.2 us: window(): values[..., offset + row_step:offset + row_step + inner_rows, offset + co...]
  transfers between devices with their start and end apart: 78 -> 0, of which waited for: 25 -> 0; matrix products, arithmetic and copies ran while one was open for 16% -> 0% of each run, Pallas kernels for 0% -> 0%
where the time goes in v1:
time: 153 us
  Pallas kernels  149 us (97%)
  local copies, waits for them, and re-layouts  3.36 us (2%)
    pallas_call x1, Pallas kernels, local(): pl.pallas_call(functools.partial(body, n_wide, n_narrow), out_shape=(jax....  149 us
    unnamed x4, local copies, waits for them, and re-layouts  3.36 us

profile of v1, /device:TPU:9, one launch (start us, length us, event | category | flops | bytes accessed | tf_op | source)
XLA Modules:
  0.0 152.6 jit_solution(2214552439809333500)
XLA Ops:
  0.6 148.5 %shard_map.77 = (f32[128,2048]{1,0:T(8,128)}, f32[2048,128]{1,0:T(8,128)}) custom-call(s32[2048]{0:T(1024)} %slot_ref.1, f32[2048,128]{1,0:T(8,128)} %design_ref.1, f32[5,128,128]{2,1,0:T(8,128)} %tiles_ref.1, s32[128,2048]{1,0:T(8,128)} %holes_ref.1, f32[128,2048]{1,0:T(8,128)} %squeeze_ref.1, f32[128,2048]{1,0:T(8,128)} %force_ref.1), custom_call_target="tpu_custom_call" | custom-call | tf_op jit(solution)/shard_map/pallas_call | solution.py:378
  149.2 0.0 copy-start
  149.2 2.4 %copy.10 = f32[128,2048]{1,0:T(8,128)} copy(f32[128,2048]{1,0:T(8,128)} %get-tuple-element.4) | data formatting | bytes 2097152
  151.6 0.0 copy-done
  151.6 1.0 copy.11
Async XLA Ops:
  149.2 2.4 %copy-start = (f32[2048,128]{1,0:T(8,128)S(1)}, f32[2048,128]{1,0:T(8,128)}, u32[]{:S(2)}) copy-start(f32[2048,128]{1,0:T(8,128)} %get-tuple-element.5) | copy-start | bytes 3145732

commit v2 on v1

--- a/solution.py
+++ b/solution.py
@@ -23,7 +23,11 @@
 GROUPS = SLOTS // GROUP
 SENT_GROUPS = SENT // GROUP
 
-DESIGN, ST_L, ST_R, ST_U, ST_D, K_L, K_R, K_U, K_D, BACK = range(10)
+DEEP = 16
+DESIGN, ST_L, ST_R, ST_U, ST_D, K_L, K_R = range(7)
+K_U = 7
+K_D = K_U + GROUPS + 1
+BACK = K_D + GROUPS + 1
 COPIES = BACK + SENT_GROUPS
 
 
@@ -100,7 +104,8 @@
     slot_ref, design_ref, tiles_ref, holes_ref, squeeze_ref, force_ref,
     pressure_ref, sens_ref,
     ext, blocks, curve, wf, wb, sums, st, st_l, st_r, k_l, k_r,
-    cond, dens, wn, ws, ww, we, src, fields, send, recv,
+    cond, dens, wn, ws, ww, we, src, ping, pong,
+    raw, raw_holes, out, send, recv, here_sem,
 ):
     w, n = lax.axis_index("wide"), lax.axis_index("narrow")
     owners = n_wide * n_narrow
@@ -116,6 +121,15 @@
     has_up, has_down = w > 0, w < n_wide - 1
     has_left, has_right = n > 0, n < n_narrow - 1
 
+    loads = [
+        pltpu.make_async_copy(squeeze_ref, raw.at[0], here_sem.at[0]),
+        pltpu.make_async_copy(force_ref, raw.at[1], here_sem.at[1]),
+        pltpu.make_async_copy(holes_ref, raw_holes, here_sem.at[2]),
+        pltpu.make_async_copy(design_ref, ext.at[pl.ds(SENT, SLOTS)], here_sem.at[3]),
+    ]
+    for load in loads:
+        load.start()
+
     barrier = pltpu.get_barrier_semaphore()
     pl.semaphore_signal(barrier, inc=1, device_id=nxt, device_id_type=MESH)
     pl.semaphore_signal(barrier, inc=1, device_id=prv, device_id_type=MESH)
@@ -136,15 +150,23 @@
     tile_rows = pl.ds(RIM, ROWS)
     top_rows, low_rows = pl.ds(RIM, RIM), pl.ds(ROWS, RIM)
     above_rows, below_rows = pl.ds(0, RIM), pl.ds(RIM + ROWS, RIM)
+    st_top, st_low = pl.ds(RIM, DEEP), pl.ds(RIM + ROWS - DEEP, DEEP)
+    st_above, st_below = pl.ds(RIM - DEEP, DEEP), pl.ds(RIM + ROWS, DEEP)
     design_copy = remote(DESIGN, design_ref.at[pl.ds(SLOTS - SENT, SENT)], ext.at[pl.ds(0, SENT)], nxt)
     st_left = remote(ST_L, st.at[:, 0, tile_rows], st_r, left)
     st_right = remote(ST_R, st.at[:, STRIPS - 1, tile_rows], st_l, right)
-    st_up = remote(ST_U, st.at[:, :, top_rows], st.at[:, :, below_rows], up)
-    st_down = remote(ST_D, st.at[:, :, low_rows], st.at[:, :, above_rows], down)
+    st_up = remote(ST_U, st.at[:, :, st_top], st.at[:, :, st_below], up)
+    st_down = remote(ST_D, st.at[:, :, st_low], st.at[:, :, st_above], down)
     k_left = remote(K_L, cond.at[0, tile_rows], k_r, left)
     k_right = remote(K_R, cond.at[STRIPS - 1, tile_rows], k_l, right)
-    k_up = remote(K_U, cond.at[:, top_rows], cond.at[:, below_rows], up)
-    k_down = remote(K_D, cond.at[:, low_rows], cond.at[:, above_rows], down)
+
+    def k_rows(c, strips):
+        return (
+            remote(K_U + c, cond.at[strips, top_rows], cond.at[strips, below_rows], up), has_up,
+            remote(K_D + c, cond.at[strips, low_rows], cond.at[strips, above_rows], down), has_down,
+        )
+
+    k_corners = k_rows(GROUPS, pl.ds(STRIPS, 1))
 
     def start_pair(first, has_first, second, has_second):
         pl.when(has_first)(first.start)
@@ -158,14 +180,15 @@
 
     design_copy.start()
 
+    for load in loads[:3]:
+        load.wait()
     for g in range(STRIPS):
         cols = pl.ds(g * 128, 128)
-        st[0, g, tile_rows, :] = squeeze_ref[:, cols]
-        st[1, g, tile_rows, :] = force_ref[:, cols]
-        st[2, g, tile_rows, :] = jnp.where(holes_ref[:, cols] > 0, 0.0, 1.0).astype(jnp.float32)
+        st[0, g, tile_rows, :] = raw[0, :, cols]
+        st[1, g, tile_rows, :] = raw[1, :, cols]
+        st[2, g, tile_rows, :] = jnp.where(raw_holes[:, cols] > 0, 0.0, 1.0).astype(jnp.float32)
     start_pair(st_left, has_left, st_right, has_right)
 
-    ext[pl.ds(SENT, SLOTS), :] = design_ref[...]
     blocks[...] = jnp.zeros(blocks.shape, jnp.float32)
     for k in range(5):
         tile = tiles_ref[k]
@@ -206,6 +229,7 @@
         stagger = stagger + (block_col // 2**level) % 2 * 4**level
         stagger = stagger + (block_row // 2**level) % 2 * (2 * 4**level)
 
+    loads[3].wait()
     design_copy.wait()
     offset = SENT - stagger
 
@@ -232,7 +256,8 @@
             total = total + jnp.where(inside[k], sums[pl.ds(k + 1, 1), :].reshape(1, 1, 128), 0.0)
         return total.reshape(count, 128)
 
-    def forward(c, _):
+    def forward(index, _):
+        c = lax.rem(index * (GROUPS - 1), GROUPS)
         take = near(c)
         lhs = jnp.concatenate([take(0, 0), take(-1, 0), take(1, 0), take(0, -1), take(0, 1)], axis=1)
         filtered = product(lhs, wf[...]) / denominator(c, 16, GROUP)
@@ -244,13 +269,15 @@
                 cond[2 * c + half, pl.ds(RIM + row * 8, 8), :] = (
                     COND_FLOOR + (1.0 - COND_FLOOR) * film * film * film
                 )
+        start_pair(*k_rows(c, pl.ds(2 * c, 2)))
+        pl.when((index == 0) & has_left)(k_left.start)
+        pl.when((index == 1) & has_right)(k_right.start)
         return 0
 
     lax.fori_loop(0, GROUPS, forward, 0)
-    start_pair(k_left, has_left, k_right, has_right)
     wait_pair(k_left, has_left, k_right, has_right)
     cond[STRIPS, tile_rows, :] = jnp.where(lane < 64, k_r[...], k_l[...])
-    start_pair(k_up, has_up, k_down, has_down)
+    start_pair(*k_corners)
 
     lane8 = lax.broadcasted_iota(jnp.int32, (8, 128), 1)
 
@@ -279,67 +306,80 @@
             for q in range(2):
                 value = jnp.where(solid, st[q, g, pl.ds(r, 8), :] * inverse, 0.0)
                 src[q, g, pl.ds(r, 8), :] = value
-                fields[0, q, g, pl.ds(r, 8), :] = value
+                ping[q, g, pl.ds(r, 8), :] = value
         return 0
 
     lax.fori_loop(4, 18, coefficients, 0)
     wait_pair(st_up, has_up, st_down, has_down)
-    wait_pair(k_up, has_up, k_down, has_down)
+
+    def rows_arrived(c, _):
+        wait_pair(*k_rows(c, pl.ds(2 * c, 2)))
+        return 0
+
+    lax.fori_loop(0, GROUPS, rows_arrived, 0)
+    wait_pair(*k_corners)
     lax.fori_loop(1, 4, coefficients, 0)
     lax.fori_loop(18, 21, coefficients, 0)
 
-    def sweep(first_step, last_step):
-        def run(index, _):
-            old, new = index % 2, (index + 1) % 2
-
-            def one(step, _):
-                r = pl.multiple_of(step * 8, 8)
-                rows = pl.ds(r, 8)
-                here = [[fields[old, q, g, rows, :] for g in range(WIDE)] for q in range(2)]
-                beside = [sides(here[q]) for q in range(2)]
-                for g in range(WIDE):
-                    a, b, c, d = wn[g, rows, :], ws[g, rows, :], ww[g, rows, :], we[g, rows, :]
-                    for q in range(2):
-                        north = fields[old, q, g, pl.ds(r - 1, 8), :]
-                        south = fields[old, q, g, pl.ds(r + 1, 8), :]
-                        west, east = beside[q][g]
-                        fields[new, q, g, rows, :] = (src[q, g, rows, :] + a * north + b * south) + (
-                            c * west + d * east
-                        )
-                return 0
-
-            lax.fori_loop(first_step, last_step, one, 0)
+    def sweep(old, new, first_step, last_step):
+        def row_of_strips(r, q):
+            rows = pl.ds(r, 8)
+            here = {g: old[q, g, rows, :] for g in (STRIPS, 0)}
+            for g in range(WIDE):
+                after = (g + 1) % WIDE
+                if after not in here:
+                    here[after] = old[q, after, rows, :]
+                west = pltpu.roll(jnp.where(lane8 == 127, here[(g + STRIPS) % WIDE], here[g]), 1, 1)
+                east = pltpu.roll(jnp.where(lane8 == 0, here[after], here[g]), 127, 1)
+                north = old[q, g, pl.ds(r - 1, 8), :]
+                south = old[q, g, pl.ds(r + 1, 8), :]
+                new[q, g, rows, :] = (
+                    src[q, g, rows, :] + wn[g, rows, :] * north + ws[g, rows, :] * south
+                ) + (ww[g, rows, :] * west + we[g, rows, :] * east)
+
+        def pair(step, _):
+            for half in range(2):
+                r = pl.multiple_of((first_step + 2 * step + half) * 8, 8)
+                for q in range(2):
+                    row_of_strips(r, q)
             return 0
 
-        return run
-
-    lax.fori_loop(0, 7, sweep(1, 21), 0)
-    lax.fori_loop(7, SWEEPS - 1, sweep(2, 20), 0)
-    last = (SWEEPS - 1) % 2
-
-    def gradient(g, _):
+        lax.fori_loop(0, (last_step - first_step) // 2, pair, 0)
+
+    def two_deep(_, carry):
+        sweep(ping, pong, 1, 21)
+        sweep(pong, ping, 1, 21)
+        return carry
+
+    def two_shallow(_, carry):
+        sweep(pong, ping, 2, 20)
+        sweep(ping, pong, 2, 20)
+        return carry
+
+    lax.fori_loop(0, 3, two_deep, 0)
+    sweep(ping, pong, 1, 21)
+    lax.fori_loop(0, (SWEEPS - 8) // 2, two_shallow, 0)
+
+    def gradient(g):
         summed = jnp.zeros((ROWS, 128), jnp.float32)
-        p = fields[last, 0, g, tile_rows, :]
-        a = fields[last, 1, g, tile_rows, :]
-        pressure_ref[:, pl.ds(pl.multiple_of(g * 128, 128), 128)] = p
+        p = pong[0, g, tile_rows, :]
+        a = pong[1, g, tile_rows, :]
+        out[:, pl.ds(g * 128 if isinstance(g, int) else pl.multiple_of(g * 128, 128), 128)] = p
         for shift in (RIM - 1, RIM + 1):
             rows = pl.ds(shift, ROWS)
-            summed = summed + (a - fields[last, 1, g, rows, :]) * (p - fields[last, 0, g, rows, :])
+            summed = summed + (a - pong[1, g, rows, :]) * (p - pong[0, g, rows, :])
         west, east = lax.rem(g + STRIPS, WIDE), g + 1
         for edge, strip, turn in ((127, west, 1), (0, east, 127)):
-            pn = pltpu.roll(jnp.where(lane == edge, fields[last, 0, strip, tile_rows, :], p), turn, 1)
-            an = pltpu.roll(jnp.where(lane == edge, fields[last, 1, strip, tile_rows, :], a), turn, 1)
+            pn = pltpu.roll(jnp.where(lane == edge, pong[0, strip, tile_rows, :], p), turn, 1)
+            an = pltpu.roll(jnp.where(lane == edge, pong[1, strip, tile_rows, :], a), turn, 1)
             summed = summed + (a - an) * (p - pn)
         density = dens[g]
         sens = -0.5 * summed * (3.0 * (1.0 - COND_FLOOR)) * density * density
         scale = denominator(g, 8, ROWS)
-        at = pl.multiple_of(8 + 8 * g, 8)
+        at = 8 + 8 * g if isinstance(g, int) else pl.multiple_of(8 + 8 * g, 8)
         for row in range(16):
             part = slice(row * 8, row * 8 + 8)
             blocks[1 + row, pl.ds(at, 8), :] = flip_block(sens[part]) / scale[part]
-        return 0
-
-    lax.fori_loop(0, STRIPS, gradient, 0)
 
     def back_copy(c):
         return remote(BACK + c, curve.at[pl.ds(c * GROUP, GROUP)], curve.at[pl.ds(SLOTS + c * GROUP, GROUP)], prv)
@@ -353,25 +393,39 @@
                 at = pl.multiple_of(at, 8)
             curve[pl.ds(at, 8), :] = value
 
-    for c in range(GROUPS):
+    def back(c, _):
+        gradient(2 * c + 1)
+        gradient(2 * c + 2)
         backward(c)
-        if c < SENT_GROUPS:
-            back_copy(c).start()
+        back_copy(c).start()
+        return 0
+
+    gradient(0)
+    lax.fori_loop(0, SENT_GROUPS, back, 0)
+    gradient(13)
+    gradient(14)
+    backward(6)
+    gradient(15)
+    pressure_copy = pltpu.make_async_copy(out, pressure_ref, here_sem.at[0])
+    pressure_copy.start()
+    backward(7)
+
+    def give(c):
+        at = c * GROUP
+        sens_ref[pl.ds(at, GROUP), :] = curve[pl.ds(stagger + at, GROUP), :]
+
     for c in range(SENT_GROUPS):
         back_copy(c).wait()
-
-    def give(c, _):
-        at = pl.multiple_of(c * GROUP, GROUP)
-        sens_ref[pl.ds(at, GROUP), :] = curve[pl.ds(stagger + c * GROUP, GROUP), :]
-        return 0
-
-    lax.fori_loop(0, GROUPS, give, 0)
+    for c in range(GROUPS):
+        give(c)
+    pressure_copy.wait()
 
 
 def solution(mesh):
     n_wide, n_narrow = mesh.shape["wide"], mesh.shape["narrow"]
     f32, bf16 = jnp.float32, jnp.bfloat16
     vmem = pl.BlockSpec(memory_space=pltpu.VMEM)
+    anywhere = pl.BlockSpec(memory_space=pl.ANY)
 
     def local(design, filter_tiles, filter_cols, slot_block, holes, squeeze_source, force_weight):
         strips = (WIDE, TALL, 128)
@@ -381,8 +435,8 @@
                 jax.ShapeDtypeStruct(holes.shape, f32),
                 jax.ShapeDtypeStruct(design.shape, f32),
             ),
-            in_specs=[pl.BlockSpec(memory_space=pltpu.SMEM)] + [vmem] * 5,
-            out_specs=(vmem, vmem),
+            in_specs=[pl.BlockSpec(memory_space=pltpu.SMEM), anywhere, vmem] + [anywhere] * 3,
+            out_specs=(anywhere, vmem),
             scratch_shapes=[
                 pltpu.VMEM((SENT + SLOTS + 8, 128), f32),
                 pltpu.VMEM((18, 144, 128), f32),
@@ -402,9 +456,14 @@
                 pltpu.VMEM(strips, f32),
                 pltpu.VMEM(strips, f32),
                 pltpu.VMEM((2,) + strips, f32),
-                pltpu.VMEM((2, 2) + strips, f32),
+                pltpu.VMEM((2,) + strips, f32),
+                pltpu.VMEM((2,) + strips, f32),
+                pltpu.VMEM((2,) + holes.shape, f32),
+                pltpu.VMEM(holes.shape, jnp.int32),
+                pltpu.VMEM(holes.shape, f32),
                 pltpu.SemaphoreType.DMA((COPIES,)),
                 pltpu.SemaphoreType.DMA((COPIES,)),
+                pltpu.SemaphoreType.DMA((4,)),
             ],
             compiler_params=pltpu.CompilerParams(
                 collective_id=0, has_side_effects=True, vmem_limit_bytes=56 * 2**20

time: 153 us -> 94.3 us (0.62)
  Pallas kernels: 149 us -> 90.1 us
    pallas_call x1, Pallas kernels: 149 us -> 90.1 us  [local(): pl.pallas_call(functools.partial(body, n_wide, n_narrow), out_shape=(jax....]
where the time goes in v2:
time: 94.3 us; the launch traced here: 94.1 us
  Pallas kernels  90.1 us (96%)
  local copies, waits for them, and re-layouts  3.36 us (4%)
    pallas_call x1, Pallas kernels, local(): pl.pallas_call(functools.partial(body, n_wide, n_narrow), out_shape=(jax....  90.1 us
    unnamed x4, local copies, waits for them, and re-layouts  3.36 us

profile of v2, /device:TPU:9, one launch (start us, length us, event | category | flops | bytes accessed | tf_op | source)
XLA Modules:
  0.0 94.1 jit_solution(17908921184162981162)
XLA Ops:
  0.6 90.1 %shard_map.77 = (f32[128,2048]{1,0:T(8,128)}, f32[2048,128]{1,0:T(8,128)}) custom-call(s32[2048]{0:T(1024)} %slot_ref.1, f32[2048,128]{1,0:T(8,128)} %design_ref.1, f32[5,128,128]{2,1,0:T(8,128)} %tiles_ref.1, s32[128,2048]{1,0:T(8,128)} %holes_ref.1, f32[128,2048]{1,0:T(8,128)} %squeeze_ref.1, f32[128,2048]{1,0:T(8,128)} %force_ref.1), custom_call_target="tpu_custom_call" | custom-call | tf_op jit(solution)/shard_map/pallas_call | solution.py:432
  90.7 0.0 copy-start
  90.7 2.4 %copy.10 = f32[128,2048]{1,0:T(8,128)} copy(f32[128,2048]{1,0:T(8,128)} %get-tuple-element.4) | data formatting | bytes 2097152
  93.1 0.0 copy-done
  93.1 1.0 %copy.11 = f32[2048,128]{1,0:T(8,128)} copy(f32[2048,128]{1,0:T(8,128)S(1)} %copy-done) | data formatting | bytes 2097152
Async XLA Ops:
  90.7 2.4 %copy-start = (f32[2048,128]{1,0:T(8,128)S(1)}, f32[2048,128]{1,0:T(8,128)}, u32[]{:S(2)}) copy-start(f32[2048,128]{1,0:T(8,128)} %get-tuple-element.5) | copy-start | bytes 3145732

commit v3 on v2

--- a/solution.py
+++ b/solution.py
@@ -148,7 +148,8 @@
         )
 
     tile_rows = pl.ds(RIM, ROWS)
-    top_rows, low_rows = pl.ds(RIM, RIM), pl.ds(ROWS, RIM)
+    k_top, k_low = pl.ds(RIM, DEEP + 1), pl.ds(RIM + ROWS - DEEP - 1, DEEP + 1)
+    k_above, k_below = pl.ds(RIM - DEEP - 1, DEEP + 1), pl.ds(RIM + ROWS, DEEP + 1)
     above_rows, below_rows = pl.ds(0, RIM), pl.ds(RIM + ROWS, RIM)
     st_top, st_low = pl.ds(RIM, DEEP), pl.ds(RIM + ROWS - DEEP, DEEP)
     st_above, st_below = pl.ds(RIM - DEEP, DEEP), pl.ds(RIM + ROWS, DEEP)
@@ -162,8 +163,8 @@
 
     def k_rows(c, strips):
         return (
-            remote(K_U + c, cond.at[strips, top_rows], cond.at[strips, below_rows], up), has_up,
-            remote(K_D + c, cond.at[strips, low_rows], cond.at[strips, above_rows], down), has_down,
+            remote(K_U + c, cond.at[strips, k_top], cond.at[strips, k_below], up), has_up,
+            remote(K_D + c, cond.at[strips, k_low], cond.at[strips, k_above], down), has_down,
         )
 
     k_corners = k_rows(GROUPS, pl.ds(STRIPS, 1))
@@ -184,9 +185,9 @@
         load.wait()
     for g in range(STRIPS):
         cols = pl.ds(g * 128, 128)
-        st[0, g, tile_rows, :] = raw[0, :, cols]
-        st[1, g, tile_rows, :] = raw[1, :, cols]
-        st[2, g, tile_rows, :] = jnp.where(raw_holes[:, cols] > 0, 0.0, 1.0).astype(jnp.float32)
+        solid = raw_holes[:, cols] <= 0
+        st[0, g, tile_rows, :] = jnp.where(solid, raw[0, :, cols], 0.0)
+        st[1, g, tile_rows, :] = jnp.where(solid, raw[1, :, cols], 0.0)
     start_pair(st_left, has_left, st_right, has_right)
 
     blocks[...] = jnp.zeros(blocks.shape, jnp.float32)
@@ -213,12 +214,12 @@
     for there, rows in ((has_up, above_rows), (has_down, below_rows)):
         @pl.when(jnp.logical_not(there))
         def _():
-            st[:, :, rows, :] = jnp.zeros((3, WIDE, RIM, 128), jnp.float32)
+            st[:, :, rows, :] = jnp.zeros((2, WIDE, RIM, 128), jnp.float32)
             cond[:, rows, :] = jnp.zeros((WIDE, RIM, 128), jnp.float32)
 
     wait_pair(st_left, has_left, st_right, has_right)
     lane = lax.broadcasted_iota(jnp.int32, (ROWS, 128), 1)
-    for q in range(3):
+    for q in range(2):
         st[q, STRIPS, tile_rows, :] = jnp.where(lane < 64, st_r[q], st_l[q])
     start_pair(st_up, has_up, st_down, has_down)
 
@@ -300,11 +301,11 @@
             west = 0.5 * (k + beside[g][0])
             east = 0.5 * (k + beside[g][1])
             inverse = 1.0 / (north + south + west + east + SQUEEZE_DAMPING)
-            solid = st[2, g, pl.ds(r, 8), :] > 0.5
+            solid = st[1, g, pl.ds(r, 8), :] > 0.0
             for ref, face in ((wn, north), (ws, south), (ww, west), (we, east)):
                 ref[g, pl.ds(r, 8), :] = jnp.where(solid, face * inverse, 0.0)
             for q in range(2):
-                value = jnp.where(solid, st[q, g, pl.ds(r, 8), :] * inverse, 0.0)
+                value = st[q, g, pl.ds(r, 8), :] * inverse
                 src[q, g, pl.ds(r, 8), :] = value
                 ping[q, g, pl.ds(r, 8), :] = value
         return 0
@@ -321,43 +322,44 @@
     lax.fori_loop(1, 4, coefficients, 0)
     lax.fori_loop(18, 21, coefficients, 0)
 
-    def sweep(old, new, first_step, last_step):
-        def row_of_strips(r, q):
+    def sweep(old, new, first_step, last_step, unroll):
+        def row_of_strips(r):
             rows = pl.ds(r, 8)
-            here = {g: old[q, g, rows, :] for g in (STRIPS, 0)}
+            here = {(q, g): old[q, g, rows, :] for q in range(2) for g in (STRIPS, 0)}
             for g in range(WIDE):
-                after = (g + 1) % WIDE
-                if after not in here:
-                    here[after] = old[q, after, rows, :]
-                west = pltpu.roll(jnp.where(lane8 == 127, here[(g + STRIPS) % WIDE], here[g]), 1, 1)
-                east = pltpu.roll(jnp.where(lane8 == 0, here[after], here[g]), 127, 1)
-                north = old[q, g, pl.ds(r - 1, 8), :]
-                south = old[q, g, pl.ds(r + 1, 8), :]
-                new[q, g, rows, :] = (
-                    src[q, g, rows, :] + wn[g, rows, :] * north + ws[g, rows, :] * south
-                ) + (ww[g, rows, :] * west + we[g, rows, :] * east)
-
-        def pair(step, _):
-            for half in range(2):
-                r = pl.multiple_of((first_step + 2 * step + half) * 8, 8)
+                before, after = (g + STRIPS) % WIDE, (g + 1) % WIDE
+                faces = [ref[g, rows, :] for ref in (wn, ws, ww, we)]
                 for q in range(2):
-                    row_of_strips(r, q)
+                    if (q, after) not in here:
+                        here[q, after] = old[q, after, rows, :]
+                    mine = here[q, g]
+                    west = pltpu.roll(jnp.where(lane8 == 127, here[q, before], mine), 1, 1)
+                    east = pltpu.roll(jnp.where(lane8 == 0, here[q, after], mine), 127, 1)
+                    north = old[q, g, pl.ds(r - 1, 8), :]
+                    south = old[q, g, pl.ds(r + 1, 8), :]
+                    new[q, g, rows, :] = (
+                        src[q, g, rows, :] + faces[0] * north + faces[1] * south
+                    ) + (faces[2] * west + faces[3] * east)
+
+        def several(step, _):
+            for part in range(unroll):
+                row_of_strips(pl.multiple_of((first_step + unroll * step + part) * 8, 8))
             return 0
 
-        lax.fori_loop(0, (last_step - first_step) // 2, pair, 0)
+        lax.fori_loop(0, (last_step - first_step) // unroll, several, 0)
 
     def two_deep(_, carry):
-        sweep(ping, pong, 1, 21)
-        sweep(pong, ping, 1, 21)
+        sweep(ping, pong, 1, 21, 4)
+        sweep(pong, ping, 1, 21, 4)
         return carry
 
     def two_shallow(_, carry):
-        sweep(pong, ping, 2, 20)
-        sweep(ping, pong, 2, 20)
+        sweep(pong, ping, 2, 20, 3)
+        sweep(ping, pong, 2, 20, 3)
         return carry
 
     lax.fori_loop(0, 3, two_deep, 0)
-    sweep(ping, pong, 1, 21)
+    sweep(ping, pong, 1, 21, 4)
     lax.fori_loop(0, (SWEEPS - 8) // 2, two_shallow, 0)
 
     def gradient(g):
@@ -444,9 +446,9 @@
                 pltpu.VMEM((640, 256), bf16),
                 pltpu.VMEM((640, 256), bf16),
                 pltpu.VMEM((8, 128), f32),
-                pltpu.VMEM((3,) + strips, f32),
-                pltpu.VMEM((3, ROWS, 128), f32),
-                pltpu.VMEM((3, ROWS, 128), f32),
+                pltpu.VMEM((2,) + strips, f32),
+                pltpu.VMEM((2, ROWS, 128), f32),
+                pltpu.VMEM((2, ROWS, 128), f32),
                 pltpu.VMEM((ROWS, 128), f32),
                 pltpu.VMEM((ROWS, 128), f32),
                 pltpu.VMEM(strips, f32),

time: 94.3 us -> 79.4 us (0.84)
  Pallas kernels: 90.1 us -> 75.2 us
    pallas_call x1, Pallas kernels: 90.1 us -> 75.2 us  [local(): pl.pallas_call(functools.partial(body, n_wide, n_narrow), out_shape=(jax....]
where the time goes in v3:
time: 79.4 us; the launch traced here: 79.2 us
  Pallas kernels  75.2 us (95%)
  local copies, waits for them, and re-layouts  3.36 us (4%)
    pallas_call x1, Pallas kernels, local(): pl.pallas_call(functools.partial(body, n_wide, n_narrow), out_shape=(jax....  75.2 us
    unnamed x4, local copies, waits for them, and re-layouts  3.36 us

profile of v3, /device:TPU:9, one launch (start us, length us, event | category | flops | bytes accessed | tf_op | source)
XLA Modules:
  0.0 79.2 jit_solution(4783476137177346695)
XLA Ops:
  0.6 75.2 %shard_map.77 = (f32[128,2048]{1,0:T(8,128)}, f32[2048,128]{1,0:T(8,128)}) custom-call(s32[2048]{0:T(1024)} %slot_ref.1, f32[2048,128]{1,0:T(8,128)} %design_ref.1, f32[5,128,128]{2,1,0:T(8,128)} %tiles_ref.1, s32[128,2048]{1,0:T(8,128)} %holes_ref.1, f32[128,2048]{1,0:T(8,128)} %squeeze_ref.1, f32[128,2048]{1,0:T(8,128)} %force_ref.1), custom_call_target="tpu_custom_call" | custom-call | tf_op jit(solution)/shard_map/pallas_call | solution.py:434
  75.8 0.0 copy-start
  75.8 2.4 %copy.10 = f32[128,2048]{1,0:T(8,128)} copy(f32[128,2048]{1,0:T(8,128)} %get-tuple-element.4) | data formatting | bytes 2097152
  78.2 0.0 copy-done
  78.2 1.0 %copy.11 = f32[2048,128]{1,0:T(8,128)} copy(f32[2048,128]{1,0:T(8,128)S(1)} %copy-done) | data formatting | bytes 2097152
Async XLA Ops:
  75.8 2.4 %copy-start = (f32[2048,128]{1,0:T(8,128)S(1)}, f32[2048,128]{1,0:T(8,128)}, u32[]{:S(2)}) copy-start(f32[2048,128]{1,0:T(8,128)} %get-tuple-element.5) | copy-start | bytes 3145732

commit v4 on v3

--- a/solution.py
+++ b/solution.py
@@ -257,8 +257,7 @@
             total = total + jnp.where(inside[k], sums[pl.ds(k + 1, 1), :].reshape(1, 1, 128), 0.0)
         return total.reshape(count, 128)
 
-    def forward(index, _):
-        c = lax.rem(index * (GROUPS - 1), GROUPS)
+    def forward(c):
         take = near(c)
         lhs = jnp.concatenate([take(0, 0), take(-1, 0), take(1, 0), take(0, -1), take(0, 1)], axis=1)
         filtered = product(lhs, wf[...]) / denominator(c, 16, GROUP)
@@ -270,12 +269,18 @@
                 cond[2 * c + half, pl.ds(RIM + row * 8, 8), :] = (
                     COND_FLOOR + (1.0 - COND_FLOOR) * film * film * film
                 )
-        start_pair(*k_rows(c, pl.ds(2 * c, 2)))
+
+    def two_forward(index, _):
+        pair = [lax.rem((2 * index + i) * (GROUPS - 1), GROUPS) for i in range(2)]
+        for c in pair:
+            forward(c)
+        for c in pair:
+            start_pair(*k_rows(c, pl.ds(2 * c, 2)))
         pl.when((index == 0) & has_left)(k_left.start)
-        pl.when((index == 1) & has_right)(k_right.start)
+        pl.when((index == 0) & has_right)(k_right.start)
         return 0
 
-    lax.fori_loop(0, GROUPS, forward, 0)
+    lax.fori_loop(0, GROUPS // 2, two_forward, 0)
     wait_pair(k_left, has_left, k_right, has_right)
     cond[STRIPS, tile_rows, :] = jnp.where(lane < 64, k_r[...], k_l[...])
     start_pair(*k_corners)
@@ -290,7 +295,7 @@
             out.append((west, east))
         return out
 
-    def coefficients(step, _):
+    def coefficients(step):
         r = pl.multiple_of(step * 8, 8)
         here = [cond[g, pl.ds(r, 8), :] for g in range(WIDE)]
         beside = sides(here)
@@ -308,9 +313,15 @@
                 value = st[q, g, pl.ds(r, 8), :] * inverse
                 src[q, g, pl.ds(r, 8), :] = value
                 ping[q, g, pl.ds(r, 8), :] = value
-        return 0
-
-    lax.fori_loop(4, 18, coefficients, 0)
+
+    def both(first, second):
+        def run(index, _):
+            coefficients(first + index)
+            coefficients(second + index)
+            return 0
+        return run
+
+    lax.fori_loop(0, 7, both(4, 11), 0)
     wait_pair(st_up, has_up, st_down, has_down)
 
     def rows_arrived(c, _):
@@ -319,8 +330,7 @@
 
     lax.fori_loop(0, GROUPS, rows_arrived, 0)
     wait_pair(*k_corners)
-    lax.fori_loop(1, 4, coefficients, 0)
-    lax.fori_loop(18, 21, coefficients, 0)
+    lax.fori_loop(0, 3, both(1, 18), 0)
 
     def sweep(old, new, first_step, last_step, unroll):
         def row_of_strips(r):
@@ -349,17 +359,17 @@
         lax.fori_loop(0, (last_step - first_step) // unroll, several, 0)
 
     def two_deep(_, carry):
-        sweep(ping, pong, 1, 21, 4)
-        sweep(pong, ping, 1, 21, 4)
+        sweep(ping, pong, 1, 21, 5)
+        sweep(pong, ping, 1, 21, 5)
         return carry
 
     def two_shallow(_, carry):
-        sweep(pong, ping, 2, 20, 3)
-        sweep(ping, pong, 2, 20, 3)
+        sweep(pong, ping, 2, 20, 6)
+        sweep(ping, pong, 2, 20, 6)
         return carry
 
     lax.fori_loop(0, 3, two_deep, 0)
-    sweep(ping, pong, 1, 21, 4)
+    sweep(ping, pong, 1, 21, 5)
     lax.fori_loop(0, (SWEEPS - 8) // 2, two_shallow, 0)
 
     def gradient(g):

time: 79.4 us -> 77 us (0.970)
  Pallas kernels: 75.2 us -> 72.7 us
    pallas_call x1, Pallas kernels: 75.2 us -> 72.7 us  [local(): pl.pallas_call(functools.partial(body, n_wide, n_narrow), out_shape=(jax....]
where the time goes in v4:
time: 77 us; the launch traced here: 76.8 us
  Pallas kernels  72.7 us (94%)
  local copies, waits for them, and re-layouts  3.36 us (4%)
    pallas_call x1, Pallas kernels, local(): pl.pallas_call(functools.partial(body, n_wide, n_narrow), out_shape=(jax....  72.7 us
    unnamed x4, local copies, waits for them, and re-layouts  3.36 us

profile of v4, /device:TPU:9, one launch (start us, length us, event | category | flops | bytes accessed | tf_op | source)
XLA Modules:
  0.0 76.8 jit_solution(4264058115824141572)
XLA Ops:
  0.6 72.7 %shard_map.77 = (f32[128,2048]{1,0:T(8,128)}, f32[2048,128]{1,0:T(8,128)}) custom-call(s32[2048]{0:T(1024)} %slot_ref.1, f32[2048,128]{1,0:T(8,128)} %design_ref.1, f32[5,128,128]{2,1,0:T(8,128)} %tiles_ref.1, s32[128,2048]{1,0:T(8,128)} %holes_ref.1, f32[128,2048]{1,0:T(8,128)} %squeeze_ref.1, f32[128,2048]{1,0:T(8,128)} %force_ref.1), custom_call_target="tpu_custom_call" | custom-call | tf_op jit(solution)/shard_map/pallas_call | solution.py:444
  73.4 0.0 copy-start
  73.4 2.4 %copy.10 = f32[128,2048]{1,0:T(8,128)} copy(f32[128,2048]{1,0:T(8,128)} %get-tuple-element.4) | data formatting | bytes 2097152
  75.8 0.0 copy-done
  75.8 1.0 %copy.11 = f32[2048,128]{1,0:T(8,128)} copy(f32[2048,128]{1,0:T(8,128)S(1)} %copy-done) | data formatting | bytes 2097152
Async XLA Ops:
  73.4 2.4 %copy-start = (f32[2048,128]{1,0:T(8,128)S(1)}, f32[2048,128]{1,0:T(8,128)}, u32[]{:S(2)}) copy-start(f32[2048,128]{1,0:T(8,128)} %get-tuple-element.5) | copy-start | bytes 3145732
